TPU v7x, 32 devices: a whole 2x2x4 slice. The times are simulated.
32 devices in a mesh: group: 2 (over y), dp: 8 (over z, x), tensor: 2 (over core).
Axes of the slice: x: 2, y: 2, z: 4, core: 2. Of those that a mesh axis runs over, the one named last changes fastest.
Arguments:
- hidden_states: bfloat16 [1, 16, 128, 8192], P(None, ('group', 'dp'), None, 'tensor'), parts along dimension 1, may hold values from -600 to 600
- up_grads: bfloat16 [1, 16, 128, 28672], P(None, ('group', 'dp'), None, 'tensor'), parts along dimension 1, may hold values from -6 to 6
- gains: bfloat16 [1, 8192], P(None, 'tensor'), may hold values from 0.25 to 1.75
- in_bases: bfloat16 [1, 8192, 64], P(None, ('tensor', 'dp')), may hold values from -0.0625 to 0.0625
- out_bases: bfloat16 [1, 28672, 64], P(None, ('tensor', 'dp')), may hold values from -0.03125 to 0.03125
- lengths: int32 [16], P(('group', 'dp')), parts along dimension 0, may hold values from 16 to 128, as said below
- queries: bfloat16 [32, 1, 4096], P(('group', 'dp')), parts along dimension 0, may hold values from -0.09375 to 0.09375
- query_ids: int32 [32], P('group'), parts along dimension 0, may hold values from 0 to 15, each once
Outputs:
- example_grads: bfloat16 [16, 1, 4096], P(('group', 'dp')), parts along dimension 0
- scores: float32 [16, 16], P(('group', 'dp')), parts along dimension 0
There are 2 independent parts, one for each index of `group`. A program takes and returns all parts, laid end to end along the dimension named above; an argument that names none is the same for every part. Nothing has to cross between parts.
Inputs may be any that keep to these rules, and one draw needn't show every extreme that they name: lengths[e] counts the leading valid tokens of example e; some example of every draw has all 128.
All inputs are finite; a program needn't handle non-finite values.
Results may differ from a plain program's by a relative error of at most 0.012.
Values may be sent and summed in bfloat16 or wider, within the bound.
A program may use at most 64 MiB of HBM per device.

v0:
```python
import math

import jax
import jax.numpy as jnp
from jax import lax
from jax.sharding import PartitionSpec as P

EPSILON = 1e-05


def local(hidden_states, up_grads, gains, in_bases, out_bases, lengths, queries, query_ids):
    layer_count, example_count, seq_len, width_local = hidden_states.shape
    hidden_local = up_grads.shape[3]
    rank_size = in_bases.shape[2]
    states = hidden_states.astype(jnp.float32)
    squares = jnp.sum(states * states, axis=3)
    power = lax.psum(squares, "tensor")
    scaled = (states * gains.astype(jnp.float32)[:, None, None, :]).astype(jnp.bfloat16)
    positions = jnp.arange(seq_len, dtype=jnp.int32)
    valid_mask = positions[None, :] < lengths[:, None]
    grad_rows = jnp.where(valid_mask[None, :, :, None], up_grads, jnp.zeros((), jnp.bfloat16))
    flat_in = scaled.reshape(layer_count, example_count * seq_len, width_local)
    flat_out = grad_rows.reshape(layer_count, example_count * seq_len, hidden_local)
    shard_in = in_bases.shape[1]
    shard_out = out_bases.shape[1]
    blocks = math.gcd(shard_in, shard_out)
    per_in = shard_in // blocks
    per_out = shard_out // blocks
    grouped_in = in_bases.reshape(layer_count, blocks, per_in * rank_size)
    grouped_out = out_bases.reshape(layer_count, blocks, per_out * rank_size)
    pieces = (
        lax.all_gather(grouped_in, "dp", axis=1, tiled=True),
        lax.all_gather(grouped_out, "dp", axis=1, tiled=True),
    )
    block_count = pieces[0].shape[1]
    rows_in = pieces[0].reshape(layer_count, block_count * per_in, rank_size)
    rows_out = pieces[1].reshape(layer_count, block_count * per_out, rank_size)
    new_in = jnp.einsum("ltd,ldr->ltr", flat_in, rows_in, preferred_element_type=jnp.float32)
    new_out = jnp.einsum("ltd,ldr->ltr", flat_out, rows_out, preferred_element_type=jnp.float32)
    proj_in = new_in
    proj_out = new_out
    proj_in, proj_out = lax.psum((proj_in, proj_out), "tensor")
    full_width = width_local * lax.axis_size("tensor")
    inverse = lax.rsqrt(power / full_width + EPSILON)
    proj_in = proj_in * inverse.reshape(layer_count, example_count * seq_len)[:, :, None]
    kronecker = jnp.einsum(
        "lesi,lesj->elij",
        proj_in.reshape(layer_count, example_count, seq_len, rank_size),
        proj_out.reshape(layer_count, example_count, seq_len, rank_size),
    )
    example_grads = (
        (kronecker * seq_len ** (-0.5))
        .reshape(example_count, layer_count, rank_size * rank_size)
        .astype(jnp.bfloat16)
    )
    flat_grads = example_grads.reshape(example_count, layer_count * rank_size * rank_size)
    in_piece = lax.all_gather(queries, "dp", axis=0, tiled=True)
    all_scores = jnp.einsum(
        "ek,qk->eq",
        flat_grads,
        in_piece.reshape(in_piece.shape[0], -1),
        preferred_element_type=jnp.float32,
    )
    scores = jnp.take(all_scores, query_ids, axis=1)
    return (example_grads, scores)


def solution(mesh):
    placed = (
        P(None, ("group", "dp"), None, "tensor"),
        P(None, ("group", "dp"), None, "tensor"),
        P(None, "tensor"),
        P(None, ("tensor", "dp"), None),
        P(None, ("tensor", "dp"), None),
        P(("group", "dp")),
        P(("group", "dp"), None, None),
        P("group"),
    )
    return jax.shard_map(
        local,
        mesh=mesh,
        in_specs=placed,
        out_specs=(P(("group", "dp"), None, None), P(("group", "dp"), None)),
        check_vma=False,
    )
```

profile of v0, /device:TPU:1, one launch (start us, length us, event | category | flops | bytes accessed | tf_op | source)
XLA Modules:
  0.0 101.6 jit_solution(9135820065976835777)
XLA Ops:
  7.2 0.0 copy-start.2
  7.2 0.0 copy-start.1
  7.2 0.0 copy-start.3
  7.2 0.0 copy-start
  7.2 0.0 all-gather.2.cloned.1.call-start
  7.3 1.3 %copy.16 = bf16[1,1792,64]{2,1,0:T(8,128)(2,1)S(1)} copy(bf16[1,1792,64]{1,2,0:T(8,128)(2,1)} %param.12) | data formatting | bytes 458752 | tf_op args[4]
  8.5 1.0 reshape.106
  9.5 0.0 all-gather.2.cloned.1.call-update
  10.2 1.0 copy.15
  11.2 0.1 reshape.102
  11.3 27.1 %all_gather.9 = bf16[1,2048,128]{2,1,0:T(8,128)(2,1)S(1)} all-gather(bf16[1,256,128]{2,1,0:T(8,128)(2,1)S(1)} %reshape.102), channel_id=1, replica_groups=mesh['group'=2,'dp'=8,'tensor'=2] {'dp'}, dimensions={1}, use_global_device_ids=true | all-gather | bytes 589824 | tf_op jit(solution)/shard_map/all_gather | solution.py:32
  38.4 0.4 reshape.103
  38.8 0.0 copy-done.2
  38.9 0.0 copy-done.1
  38.9 25.4 %all_gather.11 = bf16[16,1,4096]{2,1,0:T(2,128)(2,1)S(1)} all-gather(bf16[2,1,4096]{2,1,0:T(2,128)(2,1)S(1)} %copy.17), channel_id=1, replica_groups=mesh['group'=2,'dp'=8,'tensor'=2] {'dp'}, dimensions={0}, use_global_device_ids=true | all-gather | bytes 147456 | tf_op jit(solution)/shard_map/all_gather | solution.py:57
  64.3 0.0 copy-done.3
  64.4 0.0 copy-done
  64.4 0.3 fusion.5
  64.7 0.6 convolution_bitcast_fusion
  65.3 0.3 all-gather.2.cloned.1.call-done
  65.6 6.0 %reshape.107 = bf16[14336,64]{1,0:T(8,128)(2,1)} reshape(bf16[1,2048,448]{2,1,0:T(8,128)(2,1)} %all-gather.2.cloned.1.call-done) | data formatting | bytes 3670016 | tf_op jit(solution)/shard_map/reshape.8
  71.6 4.9 %fusion = f32[128,64]{0,1:T(8,128)S(1)} fusion(bf16[14336,64]{1,0:T(8,128)(2,1)} %reshape.107, bf16[1,1,128,14336]{3,2,1,0:T(8,128)(2,1)} %param.9, pred[128]{0:T(512)(128)(4,1)S(1)} %iota_compare_fusion), kind=kOutput, calls=%fused_computation.1 | convolution fusion | flops 236716032 | bytes 5537920 | tf_op jit(solution)/shard_map/ltd,ldr->ltr/dot_general | solution.py:39
  76.5 15.9 %all-reduce = (bf16[128,64]{0,1:T(8,128)(2,1)S(1)}, f32[1,128,64]{1,2,0:T(8,128)S(1)}, f32[1,1,128]{2,1,0:T(1,128)S(1)}) all-reduce(f32[128,64]{0,1:T(8,128)S(1)} %fusion, f32[1,128,64]{1,2,0:T(8,128)S(1)} %convolution_bitcast_fusion, f32[1,1,128]{2,1,0:T(1,128)S(1)} %bitcast.29), channel_id=1, replica_groups=mesh['group'=2,'dp'=8,'tensor'=2] {'tensor'}, use_global_device_ids=true, to_apply=%region_3.4 | all-reduce | flops 16512 | bytes 115712 | tf_op jit(solution)/shard_map/psum | solution.py:42
  92.4 0.1 fusion.7
  92.5 0.1 reshape.125
  92.6 0.7 convert_element_type.30
  93.3 0.3 convolution_bitcast_fusion.1
  93.6 0.7 gather_fusion
  94.2 0.5 fusion.16
  (6 shorter events, 0.1 us)
Async XLA Ops:
  7.2 31.7 %copy-start.2 = (bf16[1,4096]{1,0:T(2,128)(2,1)S(1)}, bf16[1,4096]{1,0:T(2,128)(2,1)}, u32[]{:S(2)}) copy-start(bf16[1,4096]{1,0:T(2,128)(2,1)} %param.10) | copy-start | bytes 24580
  7.2 31.7 %copy-start.1 = (bf16[2,1,4096]{2,0,1:T(2,128)(2,1)S(1)}, bf16[2,1,4096]{2,0,1:T(2,128)(2,1)}, u32[]{:S(2)}) copy-start(bf16[2,1,4096]{2,0,1:T(2,128)(2,1)} %param.14) | copy-start | bytes 49156
  7.2 57.1 %copy-start.3 = (s32[16]{0:T(128)S(1)}, s32[16]{0:T(128)}, u32[]{:S(2)}) copy-start(s32[16]{0:T(128)} %param.15) | copy-start | bytes 196
  7.2 57.2 %copy-start = (bf16[1,1,128,4096]{3,2,1,0:T(8,128)(2,1)S(1)}, bf16[1,1,128,4096]{3,2,1,0:T(8,128)(2,1)}, u32[]{:S(2)}) copy-start(bf16[1,1,128,4096]{3,2,1,0:T(8,128)(2,1)} %param.8) | copy-start | bytes 3145732
  7.2 58.4 %all-gather.2.cloned.1.call-start = ((), (), s32[]{:S(2)}) async-start(), calls=%async_computation | async-start | bytes 2359296 | tf_op jit(solution)/shard_map/all_gather | solution.py:33
Sparse Core Ops, SparseCore 0:
  10.2 55.3 all-gather.1
where the time goes:
time: 102 us
  blocking collectives  68.4 us (67%)
  between operations  14.8 us (15%)
  local copies, waits for them, and re-layouts  11.2 us (11%)
  matrix products  5.91 us (6%)
    all_gather x1, blocking collectives, local(): lax.all_gather(grouped_in, 'dp', axis=1, tiled=True)  27.1 us
    all_gather x1, blocking collectives, local(): in_piece = lax.all_gather(queries, 'dp', axis=0, tiled=True)  25.4 us
    psum x1, blocking collectives, local(): proj_in, proj_out = lax.psum((proj_in, proj_out), 'tensor')  15.9 us
    another operation x2, local copies, waits for them, and re-layouts  6.37 us
    dot_general x1, matrix products, local(): jnp.einsum('ltd,ldr->ltr', flat_out, rows_out, preferred_element_type=jnp...  4.92 us
    unnamed x11, local copies, waits for them, and re-layouts  2.29 us
  transfers between devices with their start and end apart: 1, of which 1 were waited for; matrix products, arithmetic and copies ran while one was open for 2% of the time, Pallas kernels for 0%

commit v1 on v0

--- a/solution.py
+++ b/solution.py
@@ -1,14 +1,17 @@
+import functools
 import math
 
 import jax
 import jax.numpy as jnp
 from jax import lax
+from jax.experimental import pallas as pl
+from jax.experimental.pallas import tpu as pltpu
 from jax.sharding import PartitionSpec as P
 
 EPSILON = 1e-05
 
 
-def local(hidden_states, up_grads, gains, in_bases, out_bases, lengths, queries, query_ids):
+def gathered_local(hidden_states, up_grads, gains, in_bases, out_bases, lengths, queries, query_ids):
     layer_count, example_count, seq_len, width_local = hidden_states.shape
     hidden_local = up_grads.shape[3]
     rank_size = in_bases.shape[2]
@@ -65,6 +68,362 @@
     return (example_grads, scores)
 
 
+def remote(src, dst, send_sem, recv_sem, where):
+    return pltpu.make_async_remote_copy(
+        src_ref=src,
+        dst_ref=dst,
+        send_sem=send_sem,
+        recv_sem=recv_sem,
+        device_id=where,
+        device_id_type=pl.DeviceIdType.MESH,
+    )
+
+
+def kernel(
+    planes,
+    hidden_ref,
+    grads_ref,
+    gains_ref,
+    in_ref,
+    out_ref,
+    lengths_ref,
+    queries_ref,
+    ids_ref,
+    flat_ref,
+    scores_ref,
+    bases,
+    hidden,
+    scaled,
+    grads,
+    sum_in,
+    sum_out,
+    power,
+    peer_power,
+    mine,
+    theirs,
+    wide,
+    all_queries,
+    local_sem,
+    z_send,
+    z_recv,
+    x_send,
+    x_recv,
+    y_send,
+    y_recv,
+    x2_send,
+    x2_recv,
+    y2_send,
+    y2_recv,
+    q_send,
+    q_recv,
+    t_send,
+    t_recv,
+):
+    group, dp, tensor = lax.axis_index("group"), lax.axis_index("dp"), lax.axis_index("tensor")
+    z, x, y = dp // 2, dp % 2, group
+    count = 2 * planes
+    x_peer, y_peer, t_peer = {"dp": 2 * z + 1 - x}, {"group": 1 - y}, {"tensor": 1 - tensor}
+    rank, wide_in, wide_out = in_ref.shape[0], in_ref.shape[1], out_ref.shape[1]
+    half, quarter = rank // 2, rank // 4
+    seq = hidden.shape[0]
+
+    own_in = pltpu.make_async_copy(in_ref, bases.at[dp, :, pl.ds(0, wide_in)], local_sem.at[0])
+    own_out = pltpu.make_async_copy(out_ref, bases.at[dp, :, pl.ds(wide_in, wide_out)], local_sem.at[1])
+    own_hidden = pltpu.make_async_copy(hidden_ref, hidden, local_sem.at[2])
+    own_grads = pltpu.make_async_copy(grads_ref, grads, local_sem.at[3])
+    own_queries = pltpu.make_async_copy(queries_ref, all_queries.at[dp], local_sem.at[4])
+    own_in.start()
+    own_out.start()
+    own_queries.start()
+    own_hidden.start()
+    own_grads.start()
+
+    barrier = pltpu.get_barrier_semaphore()
+    for step in range(1, count):
+        pl.semaphore_signal(barrier, inc=1, device_id={"dp": (dp + step) % count}, device_id_type=pl.DeviceIdType.MESH)
+    pl.semaphore_signal(barrier, inc=1, device_id=y_peer, device_id_type=pl.DeviceIdType.MESH)
+    pl.semaphore_signal(barrier, inc=1, device_id=t_peer, device_id_type=pl.DeviceIdType.MESH)
+    own_in.wait()
+    own_out.wait()
+    own_queries.wait()
+    pl.semaphore_wait(barrier, count + 1)
+
+    def rows(start, size):
+        return pl.ds(pl.multiple_of(start, quarter), size)
+
+    def part(plane, column, side):
+        return bases.at[2 * plane + column, rows(half * side, half), :]
+
+    def fourth(plane, column, side, which):
+        return bases.at[2 * plane + column, rows(half * side + quarter * which, quarter), :]
+
+    def along_z(plane, up):
+        there = {"dp": dp + 2} if up else {"dp": dp - 2}
+        ref = part(plane, x, y)
+        return remote(ref, ref, z_send.at[int(up), plane], z_recv.at[plane], there)
+
+    def over_x(plane, column):
+        ref = part(plane, column, y)
+        return remote(ref, ref, x_send.at[plane], x_recv.at[plane], x_peer)
+
+    def over_y(plane, column, side):
+        ref = part(plane, column, side)
+        return remote(ref, ref, y_send.at[plane], y_recv.at[plane], y_peer)
+
+    def second_x(plane, column, side):
+        ref = fourth(plane, column, side, 0)
+        return remote(ref, ref, x2_send.at[plane], x2_recv.at[plane], x_peer)
+
+    def second_y(plane, column, side):
+        ref = fourth(plane, column, side, 1)
+        return remote(ref, ref, y2_send.at[plane], y2_recv.at[plane], y_peer)
+
+    def to_query(step):
+        there = (dp + step) % count
+        return remote(all_queries.at[dp], all_queries.at[dp], q_send.at[step - 1], q_recv.at[dp], {"dp": there})
+
+    def multiply(unit):
+        at_in = pl.ds(pl.multiple_of(unit * wide_in, wide_in), wide_in)
+        at_out = pl.ds(pl.multiple_of(unit * wide_out, wide_out), wide_out)
+        contract = (((1,), (1,)), ((), ()))
+        sum_in[...] += lax.dot_general(
+            scaled[:, at_in], bases[unit, :, :wide_in], contract, preferred_element_type=jnp.float32
+        )
+        sum_out[...] += lax.dot_general(
+            grads[:, at_out], bases[unit, :, wide_in:], contract, preferred_element_type=jnp.float32
+        )
+
+    remote_planes = [(step, up) for step in range(1, planes) for up in (True, False)]
+
+    def place(step, up):
+        plane = z - step if up else z + step
+        return plane, (plane >= 0) if up else (plane < planes)
+
+    def onward(up):
+        return (z < planes - 1) if up else (z > 0)
+
+    @pl.when(onward(True))
+    def _():
+        along_z(z, True).start()
+
+    @pl.when(onward(False))
+    def _():
+        along_z(z, False).start()
+
+    over_x(z, x).start()
+
+    own_hidden.wait()
+    total = jnp.zeros((seq, 128), jnp.float32)
+    for start in range(0, hidden.shape[1], 128):
+        states = hidden[:, start : start + 128].astype(jnp.float32)
+        total += states * states
+        gain = gains_ref[:, start : start + 128].astype(jnp.float32)
+        scaled[:, start : start + 128] = (states * gain).astype(jnp.bfloat16)
+    power[...] = jnp.broadcast_to(jnp.sum(total, axis=1, keepdims=True), (seq, 128))
+    send_power = remote(power, peer_power, t_send.at[0], t_recv.at[0], t_peer)
+    send_power.start()
+    sum_in[...] = jnp.zeros_like(sum_in)
+    sum_out[...] = jnp.zeros_like(sum_out)
+    own_grads.wait()
+    multiply(dp)
+
+    over_x(z, 1 - x).wait_recv()
+    over_y(z, 1 - x, y).start()
+
+    def first_hops(step, up):
+        plane, there = place(step, up)
+
+        @pl.when(there)
+        def _():
+            along_z(plane, up).wait_recv()
+            if step < planes - 1:
+
+                @pl.when(onward(up))
+                def _():
+                    along_z(plane, up).start()
+
+            over_x(plane, x).start()
+            over_y(plane, x, y).start()
+
+    def second_hops(step, up):
+        plane, there = place(step, up)
+
+        @pl.when(there)
+        def _():
+            over_x(plane, 1 - x).wait_recv()
+            second_y(plane, 1 - x, y).start()
+            over_y(plane, x, 1 - y).wait_recv()
+            second_x(plane, x, 1 - y).start()
+
+    def finish(step, up):
+        plane, there = place(step, up)
+
+        @pl.when(there)
+        def _():
+            multiply(2 * plane + x)
+            second_x(plane, 1 - x, 1 - y).wait_recv()
+            second_y(plane, 1 - x, 1 - y).wait_recv()
+            multiply(2 * plane + 1 - x)
+
+    for step in range(1, planes):
+        for up in (True, False):
+            first_hops(step, up)
+        if step == 1:
+            for other in range(1, count):
+                to_query(other).start()
+            over_y(z, 1 - x, 1 - y).wait_recv()
+            multiply(2 * z + 1 - x)
+        else:
+            for up in (True, False):
+                finish(step - 1, up)
+        for up in (True, False):
+            second_hops(step, up)
+    for up in (True, False):
+        finish(planes - 1, up)
+
+    mine[0] = sum_in[...]
+    mine[1] = sum_out[...]
+    send_sums = remote(mine, theirs, t_send.at[1], t_recv.at[1], t_peer)
+    send_sums.start()
+    send_power.wait_recv()
+    mean = (power[...] + peer_power[...]) / (2 * hidden.shape[1])
+    inverse = lax.rsqrt(mean + EPSILON)[:, :rank]
+    valid = lax.broadcasted_iota(jnp.int32, (seq, rank), 0) < lengths_ref[0]
+    for other in range(1, count):
+        remote(
+            all_queries.at[dp], all_queries.at[(dp + other) % count], q_send.at[other - 1], q_recv.at[(dp + other) % count], x_peer
+        ).wait_recv()
+    send_sums.wait_recv()
+    proj_in = ((mine[0] + theirs[0]) * inverse).astype(jnp.bfloat16)
+    proj_out = jnp.where(valid, mine[1] + theirs[1], 0.0).astype(jnp.bfloat16)
+    wide[...] = lax.dot_general(
+        proj_in,
+        jnp.concatenate([proj_out, proj_out], axis=1),
+        (((0,), (0,)), ((), ())),
+        preferred_element_type=jnp.float32,
+    )
+    even = wide[pl.ds(0, half, stride=2), :]
+    odd = wide[pl.ds(1, half, stride=2), :]
+    lane = lax.broadcasted_iota(jnp.int32, (half, 2 * rank), 1)
+    flat = (jnp.where(lane < rank, even, odd) * seq ** (-0.5)).astype(jnp.bfloat16)
+    flat_ref[...] = flat
+    flat = flat.astype(jnp.float32)
+    per_device = all_queries.shape[1]
+    score = jnp.zeros((count, per_device, 128), jnp.float32)
+    for row in range(half):
+        block = all_queries[:, :, row * 128 : (row + 1) * 128].astype(jnp.float32)
+        score += block * flat[row : row + 1, :][None]
+    score = jnp.sum(score, axis=2, keepdims=True)
+    columns = ids_ref.shape[1]
+    number = per_device * lax.broadcasted_iota(jnp.int32, (count, per_device, columns), 0) + lax.broadcasted_iota(
+        jnp.int32, (count, per_device, columns), 1
+    )
+    picked = jnp.where(number == ids_ref[...][None], score, 0.0)
+    scores_ref[...] = jnp.sum(jnp.sum(picked, axis=0), axis=0, keepdims=True)
+
+    @pl.when(onward(True))
+    def _():
+        along_z(z, True).wait_send()
+
+    @pl.when(onward(False))
+    def _():
+        along_z(z, False).wait_send()
+
+    over_x(z, x).wait_send()
+    over_y(z, 1 - x, y).wait_send()
+    for step, up in remote_planes:
+        plane, there = place(step, up)
+
+        @pl.when(there)
+        def _(step=step, up=up, plane=plane):
+            if step < planes - 1:
+
+                @pl.when(onward(up))
+                def _():
+                    along_z(plane, up).wait_send()
+
+            over_x(plane, x).wait_send()
+            over_y(plane, x, y).wait_send()
+            second_y(plane, 1 - x, y).wait_send()
+            second_x(plane, x, 1 - y).wait_send()
+
+    for other in range(1, count):
+        to_query(other).wait_send()
+    send_power.wait_send()
+    send_sums.wait_send()
+
+
+def local(hidden_states, up_grads, gains, in_bases, out_bases, lengths, queries, query_ids):
+    layer_count, example_count, seq, width = hidden_states.shape
+    hidden_units = up_grads.shape[3]
+    shard_in, rank = in_bases.shape[1:]
+    shard_out = out_bases.shape[1]
+    count = lax.axis_size("dp")
+    fits = (
+        (layer_count, example_count, rank, lax.axis_size("group"), lax.axis_size("tensor")) == (1, 1, 64, 2, 2)
+        and count % 2 == 0
+        and shard_in % 128 == 0
+        and shard_out % 128 == 0
+    )
+    if not fits:
+        return gathered_local(hidden_states, up_grads, gains, in_bases, out_bases, lengths, queries, query_ids)
+    planes = count // 2
+    anywhere, vmem = pl.BlockSpec(memory_space=pl.ANY), pl.BlockSpec(memory_space=pltpu.VMEM)
+    pairs = pltpu.SemaphoreType.DMA((planes,))
+    f32, bf16 = jnp.float32, jnp.bfloat16
+    flat, scores = pl.pallas_call(
+        functools.partial(kernel, planes),
+        out_shape=(
+            jax.ShapeDtypeStruct((rank // 2, 2 * rank), bf16),
+            jax.ShapeDtypeStruct((1, query_ids.shape[0]), f32),
+        ),
+        in_specs=[anywhere, anywhere, vmem, anywhere, anywhere, pl.BlockSpec(memory_space=pltpu.SMEM), anywhere, vmem],
+        out_specs=(vmem, vmem),
+        scratch_shapes=[
+            pltpu.VMEM((count, rank, shard_in + shard_out), bf16),
+            pltpu.VMEM((seq, width), bf16),
+            pltpu.VMEM((seq, width), bf16),
+            pltpu.VMEM((seq, hidden_units), bf16),
+            pltpu.VMEM((seq, rank), f32),
+            pltpu.VMEM((seq, rank), f32),
+            pltpu.VMEM((seq, 128), f32),
+            pltpu.VMEM((seq, 128), f32),
+            pltpu.VMEM((2, seq, rank), f32),
+            pltpu.VMEM((2, seq, rank), f32),
+            pltpu.VMEM((rank, 2 * rank), f32),
+            pltpu.VMEM((count, queries.shape[0], rank * rank), bf16),
+            pltpu.SemaphoreType.DMA((5,)),
+            pltpu.SemaphoreType.DMA((2, planes)),
+            pairs,
+            pairs,
+            pairs,
+            pairs,
+            pairs,
+            pairs,
+            pairs,
+            pairs,
+            pairs,
+            pltpu.SemaphoreType.DMA((count - 1,)),
+            pltpu.SemaphoreType.DMA((count,)),
+            pltpu.SemaphoreType.DMA((2,)),
+            pltpu.SemaphoreType.DMA((2,)),
+        ],
+        compiler_params=pltpu.CompilerParams(
+            collective_id=0, has_side_effects=True, vmem_limit_bytes=48 * 1024 * 1024
+        ),
+    )(
+        hidden_states.reshape(seq, width),
+        up_grads.reshape(seq, hidden_units),
+        gains,
+        in_bases[0].T,
+        out_bases[0].T,
+        lengths,
+        queries.reshape(queries.shape[0], -1),
+        query_ids.reshape(1, -1),
+    )
+    return flat.reshape(1, 1, rank * rank), scores
+
+
 def solution(mesh):
     placed = (
         P(None, ("group", "dp"), None, "tensor"),

time: 102 us -> 48.3 us (0.47)
  blocking collectives: 68.4 us -> 0 us
  Pallas kernels: 0 us -> 38.4 us
  between operations: 14.8 us -> 1.3 us
  matrix products: 5.91 us -> 0 us
  local copies, waits for them, and re-layouts: 11.2 us -> 8.25 us
    all_gather x2 -> x0, blocking collectives: 52.5 us -> none  [the longest x1 27.1 us: local(): lax.all_gather(grouped_in, 'dp', axis=1, tiled=True)]
    pallas_call x0 -> x1, Pallas kernels: none -> 38.4 us  [local(): pl.pallas_call(functools.partial(kernel, planes), out_shape=(jax.ShapeDty...]
    psum x1 -> x0, blocking collectives: 15.9 us -> none  [local(): proj_in, proj_out = lax.psum((proj_in, proj_out), 'tensor')]
    another operation x2 -> x0, local copies, waits for them, and re-layouts: 6.37 us -> none
    dot_general x4 -> x0, matrix products: 5.91 us -> none  [the longest x1 4.92 us: local(): jnp.einsum('ltd,ldr->ltr', flat_out, rows_out, preferred_element_type=jnp...]
    unnamed x11 -> x15, local copies, waits for them, and re-layouts: 2.29 us -> 7.63 us
  transfers between devices with their start and end apart: 1 -> 0, of which waited for: 1 -> 0; matrix products, arithmetic and copies ran while one was open for 2% -> 0% of each run, Pallas kernels for 0% -> 0%
where the time goes in v1:
time: 48.3 us; the launch traced here: 47.9 us
  Pallas kernels  38.4 us (80%)
  local copies, waits for them, and re-layouts  8.25 us (17%)
  between operations  1.3 us (3%)
    pallas_call x1, Pallas kernels, local(): pl.pallas_call(functools.partial(kernel, planes), out_shape=(jax.ShapeDty...  38.4 us
    unnamed x15, local copies, waits for them, and re-layouts  7.63 us

profile of v1, /device:TPU:1, one launch (start us, length us, event | category | flops | bytes accessed | tf_op | source)
XLA Modules:
  0.0 47.9 jit_solution(10492245893572297734)
XLA Ops:
  1.3 0.0 copy-start
  1.3 2.0 %copy-done = bf16[1,1,128,14336]{3,2,1,0:T(8,128)(2,1)S(1)} copy-done((bf16[1,1,128,14336]{3,2,1,0:T(8,128)(2,1)S(1)}, bf16[1,1,128,14336]{3,2,1,0:T(8,128)(2,1)}, u32[]{:S(2)}) %copy-start) | copy-done | bytes 3670040
  3.3 0.0 copy-start.1
  3.3 1.2 %copy-done.1 = bf16[1,1,128,4096]{3,2,1,0:T(8,128)(2,1)S(1)} copy-done((bf16[1,1,128,4096]{3,2,1,0:T(8,128)(2,1)S(1)}, bf16[1,1,128,4096]{3,2,1,0:T(8,128)(2,1)}, u32[]{:S(2)}) %copy-start.1) | copy-done | bytes 1048600
  4.5 0.0 copy-start.2
  4.5 0.9 %copy-done.2 = bf16[1,1792,64]{1,2,0:T(8,128)(2,1)S(1)} copy-done((bf16[1,1792,64]{1,2,0:T(8,128)(2,1)S(1)}, bf16[1,1792,64]{1,2,0:T(8,128)(2,1)}, u32[]{:S(2)}) %copy-start.2) | copy-done | bytes 229400
  5.5 0.0 copy-start.3
  5.5 0.8 %copy-done.3 = bf16[1,512,64]{1,2,0:T(8,128)(2,1)S(1)} copy-done((bf16[1,512,64]{1,2,0:T(8,128)(2,1)S(1)}, bf16[1,512,64]{1,2,0:T(8,128)(2,1)}, u32[]{:S(2)}) %copy-start.3) | copy-done | bytes 65560
  6.3 0.0 copy-start.4
  6.3 0.7 %copy-done.4 = bf16[1,4096]{1,0:T(2,128)(2,1)S(1)} copy-done((bf16[1,4096]{1,0:T(2,128)(2,1)S(1)}, bf16[1,4096]{1,0:T(2,128)(2,1)}, u32[]{:S(2)}) %copy-start.4) | copy-done | bytes 8216
  7.0 0.0 copy-start.5
  7.0 0.7 %copy-done.5 = bf16[2,1,4096]{2,0,1:T(2,128)(2,1)S(1)} copy-done((bf16[2,1,4096]{2,0,1:T(2,128)(2,1)S(1)}, bf16[2,1,4096]{2,0,1:T(2,128)(2,1)}, u32[]{:S(2)}) %copy-start.5) | copy-done | bytes 16408
  7.8 0.0 copy-start.6
  7.8 0.7 %copy-done.6 = s32[16]{0:T(128)S(1)} copy-done((s32[16]{0:T(128)S(1)}, s32[16]{0:T(128)}, u32[]{:S(2)}) %copy-start.6) | copy-done | bytes 88
  8.4 38.4 %shard_map.95 = (bf16[32,128]{1,0:T(8,128)(2,1)S(1)}, f32[1,16]{1,0:T(1,128)S(1)}) custom-call(bf16[128,4096]{1,0:T(8,128)(2,1)S(1)} %bitcast.11, bf16[128,14336]{1,0:T(8,128)(2,1)S(1)} %bitcast.10, bf16[1,4096]{1,0:T(2,128)(2,1)S(1)} %copy-done.4, bf16[64,512]{1,0:T(8,128)(2,1)S(1)} %bitcast.13, bf16[64,1792]{1,0:T(8,128)(2,1)S(1)} %bitcast.12, ...), custom_call_target="tpu_custom_call" | custom-call | tf_op jit(solution)/shard_map/pallas_call | solution.py:374
  46.8 0.6 %reshape.23 = bf16[1,1,4096]{2,1,0:T(2,128)(2,1)} reshape(bf16[32,128]{1,0:T(8,128)(2,1)S(1)} %get-tuple-element.4) | data formatting | bytes 16384 | tf_op jit(solution)/shard_map/reshape | solution.py:424
  47.4 0.5 %copy.12 = f32[1,16]{1,0:T(1,128)} copy(f32[1,16]{1,0:T(1,128)S(1)} %get-tuple-element.9) | data formatting | bytes 128
Async XLA Ops:
  1.3 2.0 %copy-start = (bf16[1,1,128,14336]{3,2,1,0:T(8,128)(2,1)S(1)}, bf16[1,1,128,14336]{3,2,1,0:T(8,128)(2,1)}, u32[]{:S(2)}) copy-start(bf16[1,1,128,14336]{3,2,1,0:T(8,128)(2,1)} %param.9) | copy-start | bytes 11010052
  3.3 1.2 %copy-start.1 = (bf16[1,1,128,4096]{3,2,1,0:T(8,128)(2,1)S(1)}, bf16[1,1,128,4096]{3,2,1,0:T(8,128)(2,1)}, u32[]{:S(2)}) copy-start(bf16[1,1,128,4096]{3,2,1,0:T(8,128)(2,1)} %param.8) | copy-start | bytes 3145732
  4.5 0.9 %copy-start.2 = (bf16[1,1792,64]{1,2,0:T(8,128)(2,1)S(1)}, bf16[1,1792,64]{1,2,0:T(8,128)(2,1)}, u32[]{:S(2)}) copy-start(bf16[1,1792,64]{1,2,0:T(8,128)(2,1)} %param.12) | copy-start | bytes 688132
  5.5 0.8 %copy-start.3 = (bf16[1,512,64]{1,2,0:T(8,128)(2,1)S(1)}, bf16[1,512,64]{1,2,0:T(8,128)(2,1)}, u32[]{:S(2)}) copy-start(bf16[1,512,64]{1,2,0:T(8,128)(2,1)} %param.11) | copy-start | bytes 196612
  6.3 0.7 %copy-start.4 = (bf16[1,4096]{1,0:T(2,128)(2,1)S(1)}, bf16[1,4096]{1,0:T(2,128)(2,1)}, u32[]{:S(2)}) copy-start(bf16[1,4096]{1,0:T(2,128)(2,1)} %gains_ref.1) | copy-start | bytes 24580
  7.0 0.7 %copy-start.5 = (bf16[2,1,4096]{2,0,1:T(2,128)(2,1)S(1)}, bf16[2,1,4096]{2,0,1:T(2,128)(2,1)}, u32[]{:S(2)}) copy-start(bf16[2,1,4096]{2,0,1:T(2,128)(2,1)} %param.14) | copy-start | bytes 49156
  7.8 0.7 %copy-start.6 = (s32[16]{0:T(128)S(1)}, s32[16]{0:T(128)}, u32[]{:S(2)}) copy-start(s32[16]{0:T(128)} %param.15) | copy-start | bytes 196

commit v2 on v1

--- a/solution.py
+++ b/solution.py
@@ -81,14 +81,17 @@
 
 def kernel(
     planes,
+    chunks,
+    lag,
+    late,
     hidden_ref,
     grads_ref,
-    gains_ref,
+    gains_hbm,
     in_ref,
     out_ref,
-    lengths_ref,
+    lengths_hbm,
     queries_ref,
-    ids_ref,
+    ids_hbm,
     flat_ref,
     scores_ref,
     bases,
@@ -103,6 +106,9 @@
     theirs,
     wide,
     all_queries,
+    gains_ref,
+    lengths_ref,
+    ids_ref,
     local_sem,
     z_send,
     z_recv,
@@ -125,6 +131,7 @@
     x_peer, y_peer, t_peer = {"dp": 2 * z + 1 - x}, {"group": 1 - y}, {"tensor": 1 - tensor}
     rank, wide_in, wide_out = in_ref.shape[0], in_ref.shape[1], out_ref.shape[1]
     half, quarter = rank // 2, rank // 4
+    width = (wide_in + wide_out) // chunks
     seq = hidden.shape[0]
 
     own_in = pltpu.make_async_copy(in_ref, bases.at[dp, :, pl.ds(0, wide_in)], local_sem.at[0])
@@ -132,9 +139,15 @@
     own_hidden = pltpu.make_async_copy(hidden_ref, hidden, local_sem.at[2])
     own_grads = pltpu.make_async_copy(grads_ref, grads, local_sem.at[3])
     own_queries = pltpu.make_async_copy(queries_ref, all_queries.at[dp], local_sem.at[4])
+    own_gains = pltpu.make_async_copy(gains_hbm, gains_ref, local_sem.at[5])
+    own_lengths = pltpu.make_async_copy(lengths_hbm, lengths_ref, local_sem.at[6])
+    own_ids = pltpu.make_async_copy(ids_hbm, ids_ref, local_sem.at[7])
     own_in.start()
     own_out.start()
+    own_gains.start()
     own_queries.start()
+    own_lengths.start()
+    own_ids.start()
     own_hidden.start()
     own_grads.start()
 
@@ -151,47 +164,50 @@
     def rows(start, size):
         return pl.ds(pl.multiple_of(start, quarter), size)
 
-    def part(plane, column, side):
-        return bases.at[2 * plane + column, rows(half * side, half), :]
-
-    def fourth(plane, column, side, which):
-        return bases.at[2 * plane + column, rows(half * side + quarter * which, quarter), :]
-
-    def along_z(plane, up):
+    def columns(chunk):
+        return pl.ds(chunk * width, width)
+
+    def part(plane, column, side, chunk):
+        return bases.at[2 * plane + column, rows(half * side, half), columns(chunk)]
+
+    def fourth(plane, column, side, which, chunk):
+        return bases.at[2 * plane + column, rows(half * side + quarter * which, quarter), columns(chunk)]
+
+    def along_z(plane, up, c):
         there = {"dp": dp + 2} if up else {"dp": dp - 2}
-        ref = part(plane, x, y)
-        return remote(ref, ref, z_send.at[int(up), plane], z_recv.at[plane], there)
-
-    def over_x(plane, column):
-        ref = part(plane, column, y)
-        return remote(ref, ref, x_send.at[plane], x_recv.at[plane], x_peer)
-
-    def over_y(plane, column, side):
-        ref = part(plane, column, side)
-        return remote(ref, ref, y_send.at[plane], y_recv.at[plane], y_peer)
-
-    def second_x(plane, column, side):
-        ref = fourth(plane, column, side, 0)
-        return remote(ref, ref, x2_send.at[plane], x2_recv.at[plane], x_peer)
-
-    def second_y(plane, column, side):
-        ref = fourth(plane, column, side, 1)
-        return remote(ref, ref, y2_send.at[plane], y2_recv.at[plane], y_peer)
+        ref = part(plane, x, y, c)
+        return remote(ref, ref, z_send.at[int(up), plane, c], z_recv.at[plane, c], there)
+
+    def over_x(plane, column, c):
+        ref = part(plane, column, y, c)
+        return remote(ref, ref, x_send.at[plane, c], x_recv.at[plane, c], x_peer)
+
+    def over_y(plane, column, side, c):
+        ref = part(plane, column, side, c)
+        return remote(ref, ref, y_send.at[plane, c], y_recv.at[plane, c], y_peer)
+
+    def second_x(plane, column, side, c):
+        ref = fourth(plane, column, side, 0, c)
+        return remote(ref, ref, x2_send.at[plane, c], x2_recv.at[plane, c], x_peer)
+
+    def second_y(plane, column, side, c):
+        ref = fourth(plane, column, side, 1, c)
+        return remote(ref, ref, y2_send.at[plane, c], y2_recv.at[plane, c], y_peer)
 
     def to_query(step):
         there = (dp + step) % count
         return remote(all_queries.at[dp], all_queries.at[dp], q_send.at[step - 1], q_recv.at[dp], {"dp": there})
 
-    def multiply(unit):
-        at_in = pl.ds(pl.multiple_of(unit * wide_in, wide_in), wide_in)
-        at_out = pl.ds(pl.multiple_of(unit * wide_out, wide_out), wide_out)
+    def multiply(unit, chunk):
         contract = (((1,), (1,)), ((), ()))
-        sum_in[...] += lax.dot_general(
-            scaled[:, at_in], bases[unit, :, :wide_in], contract, preferred_element_type=jnp.float32
-        )
-        sum_out[...] += lax.dot_general(
-            grads[:, at_out], bases[unit, :, wide_in:], contract, preferred_element_type=jnp.float32
-        )
+        low, high = chunk * width, (chunk + 1) * width
+        for into, values, start, size in ((sum_in, scaled, 0, wide_in), (sum_out, grads, wide_in, wide_out)):
+            first, last = max(low, start), min(high, start + size)
+            if first < last:
+                at = pl.ds(pl.multiple_of(unit * size + (first - start), 128), last - first)
+                into[...] += lax.dot_general(
+                    values[:, at], bases[unit, :, first:last], contract, preferred_element_type=jnp.float32
+                )
 
     remote_planes = [(step, up) for step in range(1, planes) for up in (True, False)]
 
@@ -202,16 +218,19 @@
     def onward(up):
         return (z < planes - 1) if up else (z > 0)
 
-    @pl.when(onward(True))
-    def _():
-        along_z(z, True).start()
-
-    @pl.when(onward(False))
-    def _():
-        along_z(z, False).start()
-
-    over_x(z, x).start()
-
+    for c in range(chunks):
+
+        @pl.when(onward(True))
+        def _(c=c):
+            along_z(z, True, c).start()
+
+        @pl.when(onward(False))
+        def _(c=c):
+            along_z(z, False, c).start()
+
+        over_x(z, x, c).start()
+
+    own_gains.wait()
     own_hidden.wait()
     total = jnp.zeros((seq, 128), jnp.float32)
     for start in range(0, hidden.shape[1], 128):
@@ -225,61 +244,66 @@
     sum_in[...] = jnp.zeros_like(sum_in)
     sum_out[...] = jnp.zeros_like(sum_out)
     own_grads.wait()
-    multiply(dp)
-
-    over_x(z, 1 - x).wait_recv()
-    over_y(z, 1 - x, y).start()
-
-    def first_hops(step, up):
+    for c in range(chunks):
+        multiply(dp, c)
+
+    def first_hop(step, up, c):
         plane, there = place(step, up)
 
         @pl.when(there)
         def _():
-            along_z(plane, up).wait_recv()
+            along_z(plane, up, c).wait_recv()
             if step < planes - 1:
 
                 @pl.when(onward(up))
                 def _():
-                    along_z(plane, up).start()
-
-            over_x(plane, x).start()
-            over_y(plane, x, y).start()
-
-    def second_hops(step, up):
+                    along_z(plane, up, c).start()
+
+            over_x(plane, x, c).start()
+            over_y(plane, x, y, c).start()
+
+    def second_hop(step, up, c):
         plane, there = place(step, up)
 
         @pl.when(there)
         def _():
-            over_x(plane, 1 - x).wait_recv()
-            second_y(plane, 1 - x, y).start()
-            over_y(plane, x, 1 - y).wait_recv()
-            second_x(plane, x, 1 - y).start()
-
-    def finish(step, up):
+            over_x(plane, 1 - x, c).wait_recv()
+            second_y(plane, 1 - x, y, c).start()
+            over_y(plane, x, 1 - y, c).wait_recv()
+            second_x(plane, x, 1 - y, c).start()
+            multiply(2 * plane + x, c)
+
+    def finish(step, up, c):
         plane, there = place(step, up)
 
         @pl.when(there)
         def _():
-            multiply(2 * plane + x)
-            second_x(plane, 1 - x, 1 - y).wait_recv()
-            second_y(plane, 1 - x, 1 - y).wait_recv()
-            multiply(2 * plane + 1 - x)
-
-    for step in range(1, planes):
-        for up in (True, False):
-            first_hops(step, up)
-        if step == 1:
+            second_x(plane, 1 - x, 1 - y, c).wait_recv()
+            second_y(plane, 1 - x, 1 - y, c).wait_recv()
+            multiply(2 * plane + 1 - x, c)
+
+    slots = (planes - 1) * chunks
+    for slot in range(slots + lag + late):
+        if slot < slots:
+            for up in (True, False):
+                first_hop(slot // chunks + 1, up, slot % chunks)
+        if slot == chunks:
             for other in range(1, count):
                 to_query(other).start()
-            over_y(z, 1 - x, 1 - y).wait_recv()
-            multiply(2 * z + 1 - x)
-        else:
+        again = slot - lag
+        if -chunks <= again < 0:
+            over_x(z, 1 - x, again + chunks).wait_recv()
+            over_y(z, 1 - x, y, again + chunks).start()
+        elif 0 <= again < slots:
             for up in (True, False):
-                finish(step - 1, up)
-        for up in (True, False):
-            second_hops(step, up)
-    for up in (True, False):
-        finish(planes - 1, up)
+                second_hop(again // chunks + 1, up, again % chunks)
+        last = slot - lag - late
+        if -chunks <= last < 0:
+            over_y(z, 1 - x, 1 - y, last + chunks).wait_recv()
+            multiply(2 * z + 1 - x, last + chunks)
+        elif 0 <= last < slots:
+            for up in (True, False):
+                finish(last // chunks + 1, up, last % chunks)
 
     mine[0] = sum_in[...]
     mine[1] = sum_out[...]
@@ -288,6 +312,8 @@
     send_power.wait_recv()
     mean = (power[...] + peer_power[...]) / (2 * hidden.shape[1])
     inverse = lax.rsqrt(mean + EPSILON)[:, :rank]
+    own_lengths.wait()
+    own_ids.wait()
     valid = lax.broadcasted_iota(jnp.int32, (seq, rank), 0) < lengths_ref[0]
     for other in range(1, count):
         remote(
@@ -314,38 +340,40 @@
         block = all_queries[:, :, row * 128 : (row + 1) * 128].astype(jnp.float32)
         score += block * flat[row : row + 1, :][None]
     score = jnp.sum(score, axis=2, keepdims=True)
-    columns = ids_ref.shape[1]
-    number = per_device * lax.broadcasted_iota(jnp.int32, (count, per_device, columns), 0) + lax.broadcasted_iota(
-        jnp.int32, (count, per_device, columns), 1
+    places = ids_ref.shape[1]
+    number = per_device * lax.broadcasted_iota(jnp.int32, (count, per_device, places), 0) + lax.broadcasted_iota(
+        jnp.int32, (count, per_device, places), 1
     )
     picked = jnp.where(number == ids_ref[...][None], score, 0.0)
     scores_ref[...] = jnp.sum(jnp.sum(picked, axis=0), axis=0, keepdims=True)
 
-    @pl.when(onward(True))
-    def _():
-        along_z(z, True).wait_send()
-
-    @pl.when(onward(False))
-    def _():
-        along_z(z, False).wait_send()
-
-    over_x(z, x).wait_send()
-    over_y(z, 1 - x, y).wait_send()
-    for step, up in remote_planes:
-        plane, there = place(step, up)
-
-        @pl.when(there)
-        def _(step=step, up=up, plane=plane):
-            if step < planes - 1:
-
-                @pl.when(onward(up))
-                def _():
-                    along_z(plane, up).wait_send()
-
-            over_x(plane, x).wait_send()
-            over_y(plane, x, y).wait_send()
-            second_y(plane, 1 - x, y).wait_send()
-            second_x(plane, x, 1 - y).wait_send()
+    for c in range(chunks):
+
+        @pl.when(onward(True))
+        def _(c=c):
+            along_z(z, True, c).wait_send()
+
+        @pl.when(onward(False))
+        def _(c=c):
+            along_z(z, False, c).wait_send()
+
+        over_x(z, x, c).wait_send()
+        over_y(z, 1 - x, y, c).wait_send()
+        for step, up in remote_planes:
+            plane, there = place(step, up)
+
+            @pl.when(there)
+            def _(step=step, up=up, plane=plane, c=c):
+                if step < planes - 1:
+
+                    @pl.when(onward(up))
+                    def _():
+                        along_z(plane, up, c).wait_send()
+
+                over_x(plane, x, c).wait_send()
+                over_y(plane, x, y, c).wait_send()
+                second_y(plane, 1 - x, y, c).wait_send()
+                second_x(plane, x, 1 - y, c).wait_send()
 
     for other in range(1, count):
         to_query(other).wait_send()
@@ -368,16 +396,18 @@
     if not fits:
         return gathered_local(hidden_states, up_grads, gains, in_bases, out_bases, lengths, queries, query_ids)
     planes = count // 2
-    anywhere, vmem = pl.BlockSpec(memory_space=pl.ANY), pl.BlockSpec(memory_space=pltpu.VMEM)
-    pairs = pltpu.SemaphoreType.DMA((planes,))
+    tiles = (shard_in + shard_out) // 128
+    chunks = 3 if tiles % 3 == 0 else 1
+    hbm, vmem = pl.BlockSpec(memory_space=pltpu.HBM), pl.BlockSpec(memory_space=pltpu.VMEM)
+    pairs = pltpu.SemaphoreType.DMA((planes, chunks))
     f32, bf16 = jnp.float32, jnp.bfloat16
     flat, scores = pl.pallas_call(
-        functools.partial(kernel, planes),
+        functools.partial(kernel, planes, chunks, chunks + 1, chunks),
         out_shape=(
             jax.ShapeDtypeStruct((rank // 2, 2 * rank), bf16),
             jax.ShapeDtypeStruct((1, query_ids.shape[0]), f32),
         ),
-        in_specs=[anywhere, anywhere, vmem, anywhere, anywhere, pl.BlockSpec(memory_space=pltpu.SMEM), anywhere, vmem],
+        in_specs=[hbm] * 8,
         out_specs=(vmem, vmem),
         scratch_shapes=[
             pltpu.VMEM((count, rank, shard_in + shard_out), bf16),
@@ -392,8 +422,11 @@
             pltpu.VMEM((2, seq, rank), f32),
             pltpu.VMEM((rank, 2 * rank), f32),
             pltpu.VMEM((count, queries.shape[0], rank * rank), bf16),
-            pltpu.SemaphoreType.DMA((5,)),
-            pltpu.SemaphoreType.DMA((2, planes)),
+            pltpu.VMEM((1, width), bf16),
+            pltpu.SMEM(lengths.shape, jnp.int32),
+            pltpu.VMEM((1, query_ids.shape[0]), jnp.int32),
+            pltpu.SemaphoreType.DMA((8,)),
+            pltpu.SemaphoreType.DMA((2, planes, chunks)),
             pairs,
             pairs,
             pairs,
@@ -409,7 +442,7 @@
             pltpu.SemaphoreType.DMA((2,)),
         ],
         compiler_params=pltpu.CompilerParams(
-            collective_id=0, has_side_effects=True, vmem_limit_bytes=48 * 1024 * 1024
+            collective_id=0, has_side_effects=True, vmem_limit_bytes=64 * 1024 * 1024
         ),
     )(
         hidden_states.reshape(seq, width),

time: 48.3 us -> 36.3 us (0.75)
  Pallas kernels: 38.4 us -> 32.4 us
  local copies, waits for them, and re-layouts: 8.25 us -> 2.45 us
    unnamed x15 -> x1, local copies, waits for them, and re-layouts: 7.63 us -> 1.14 us
    pallas_call x1, Pallas kernels: 38.4 us -> 32.4 us  [local(): pl.pallas_call(functools.partial(kernel, planes, chunks, chunks + 1, chun...]
    reshape x1, local copies, waits for them, and re-layouts: 0.62 us -> 1.31 us  [local(): return (flat.reshape(1, 1, rank * rank), scores)]
where the time goes in v2:
time: 36.3 us; the launch traced here: 36.1 us
  Pallas kernels  32.4 us (89%)
  local copies, waits for them, and re-layouts  2.45 us (7%)
  between operations  1.29 us (4%)
    pallas_call x1, Pallas kernels, local(): pl.pallas_call(functools.partial(kernel, planes, chunks, chunks + 1, chun...  32.4 us
    reshape x1, local copies, waits for them, and re-layouts, local(): return (flat.reshape(1, 1, rank * rank), scores)  1.31 us
    unnamed x1, local copies, waits for them, and re-layouts  1.14 us

profile of v2, /device:TPU:1, one launch (start us, length us, event | category | flops | bytes accessed | tf_op | source)
XLA Modules:
  0.0 36.1 jit_solution(8381195089454056323)
XLA Ops:
  1.3 32.4 %shard_map.95 = (bf16[32,128]{1,0:T(8,128)(2,1)}, f32[1,16]{1,0:T(1,128)}) custom-call(bf16[128,4096]{1,0:T(8,128)(2,1)} %bitcast.11, bf16[128,14336]{1,0:T(8,128)(2,1)} %bitcast.10, bf16[1,4096]{1,0:T(2,128)(2,1)} %gains_hbm.1, bf16[64,512]{1,0:T(8,128)(2,1)} %bitcast.13, bf16[64,1792]{1,0:T(8,128)(2,1)} %bitcast.12, s32[1]{0:T(128)S(6)} %copy.11.lengths_hbm, ...), custom_call_target="tpu_custom_call" | custom-call | tf_op jit(solution)/shard_map/pallas_call | solution.py:404
  33.7 1.3 %reshape.23 = bf16[1,1,4096]{2,1,0:T(2,128)(2,1)} reshape(bf16[32,128]{1,0:T(8,128)(2,1)} %get-tuple-element.4) | data formatting | bytes 16384 | tf_op jit(solution)/shard_map/reshape | solution.py:457
  35.0 1.1 %copy.12 = f32[1,16]{1,0:T(1,128)} copy(f32[1,16]{1,0:T(1,128)} %get-tuple-element.9) | data formatting | bytes 128

commit v3 on v2

--- a/solution.py
+++ b/solution.py
@@ -67,6 +67,10 @@
     scores = jnp.take(all_scores, query_ids, axis=1)
     return (example_grads, scores)
 
+WAYS = ("NMT", "MMT", "MNT")
+TILES = (6, 6, 6)
+LAG, LATE, ASK = 3, 5, 3
+
 
 def remote(src, dst, send_sem, recv_sem, where):
     return pltpu.make_async_remote_copy(
@@ -81,9 +85,11 @@
 
 def kernel(
     planes,
-    chunks,
+    widths,
+    ways,
     lag,
     late,
+    ask,
     hidden_ref,
     grads_ref,
     gains_hbm,
@@ -92,8 +98,7 @@
     lengths_hbm,
     queries_ref,
     ids_hbm,
-    flat_ref,
-    scores_ref,
+    packed_ref,
     bases,
     hidden,
     scaled,
@@ -131,7 +136,8 @@
     x_peer, y_peer, t_peer = {"dp": 2 * z + 1 - x}, {"group": 1 - y}, {"tensor": 1 - tensor}
     rank, wide_in, wide_out = in_ref.shape[0], in_ref.shape[1], out_ref.shape[1]
     half, quarter = rank // 2, rank // 4
-    width = (wide_in + wide_out) // chunks
+    chunks = len(widths)
+    edges = [sum(widths[:c]) for c in range(chunks + 1)]
     seq = hidden.shape[0]
 
     own_in = pltpu.make_async_copy(in_ref, bases.at[dp, :, pl.ds(0, wide_in)], local_sem.at[0])
@@ -165,7 +171,10 @@
         return pl.ds(pl.multiple_of(start, quarter), size)
 
     def columns(chunk):
-        return pl.ds(chunk * width, width)
+        return pl.ds(edges[chunk], widths[chunk])
+
+    def shard(plane, column, chunk):
+        return bases.at[2 * plane + column, :, columns(chunk)]
 
     def part(plane, column, side, chunk):
         return bases.at[2 * plane + column, rows(half * side, half), columns(chunk)]
@@ -173,13 +182,13 @@
     def fourth(plane, column, side, which, chunk):
         return bases.at[2 * plane + column, rows(half * side + quarter * which, quarter), columns(chunk)]
 
-    def along_z(plane, up, c):
+    def along_z(plane, up, c, whole):
         there = {"dp": dp + 2} if up else {"dp": dp - 2}
-        ref = part(plane, x, y, c)
+        ref = shard(plane, x, c) if whole else part(plane, x, y, c)
         return remote(ref, ref, z_send.at[int(up), plane, c], z_recv.at[plane, c], there)
 
-    def over_x(plane, column, c):
-        ref = part(plane, column, y, c)
+    def over_x(plane, column, c, whole=False):
+        ref = shard(plane, column, c) if whole else part(plane, column, y, c)
         return remote(ref, ref, x_send.at[plane, c], x_recv.at[plane, c], x_peer)
 
     def over_y(plane, column, side, c):
@@ -190,8 +199,8 @@
         ref = fourth(plane, column, side, 0, c)
         return remote(ref, ref, x2_send.at[plane, c], x2_recv.at[plane, c], x_peer)
 
-    def second_y(plane, column, side, c):
-        ref = fourth(plane, column, side, 1, c)
+    def second_y(plane, column, side, c, way):
+        ref = fourth(plane, column, side, 1, c) if way == "N" else part(plane, column, side, c)
         return remote(ref, ref, y2_send.at[plane, c], y2_recv.at[plane, c], y_peer)
 
     def to_query(step):
@@ -200,7 +209,7 @@
 
     def multiply(unit, chunk):
         contract = (((1,), (1,)), ((), ()))
-        low, high = chunk * width, (chunk + 1) * width
+        low, high = edges[chunk], edges[chunk + 1]
         for into, values, start, size in ((sum_in, scaled, 0, wide_in), (sum_out, grads, wide_in, wide_out)):
             first, last = max(low, start), min(high, start + size)
             if first < last:
@@ -218,17 +227,53 @@
     def onward(up):
         return (z < planes - 1) if up else (z > 0)
 
+    def on_z(plane, step, up, c, do):
+        takers = [far for far in range(step, planes) if ways[far - 1][c] in "FT"]
+        if not takers or takers[0] == step:
+            do(along_z(plane, up, c, bool(takers)))
+            return
+        last = (plane + takers[0] < planes) if up else (plane >= takers[0])
+
+        @pl.when(last)
+        def _():
+            do(along_z(plane, up, c, True))
+
+        @pl.when(jnp.logical_not(last))
+        def _():
+            do(along_z(plane, up, c, False))
+
+    def own_sends(c, do):
+        for up in (True, False):
+
+            @pl.when(onward(up))
+            def _(up=up):
+                on_z(z, 1, up, c, do)
+
+        do(over_x(z, x, c))
+
+    def first_sends(plane, step, up, c, do):
+        way = ways[step - 1][c]
+        if step < planes - 1:
+
+            @pl.when(onward(up))
+            def _():
+                on_z(plane, step + 1, up, c, do)
+
+        do(over_x(plane, x, c, way == "T"))
+        if way in "NM":
+            do(over_y(plane, x, y, c))
+
+    def begin(copy):
+        copy.start()
+
+    def arrived(copy):
+        copy.wait_recv()
+
+    def sent(copy):
+        copy.wait_send()
+
     for c in range(chunks):
-
-        @pl.when(onward(True))
-        def _(c=c):
-            along_z(z, True, c).start()
-
-        @pl.when(onward(False))
-        def _(c=c):
-            along_z(z, False, c).start()
-
-        over_x(z, x, c).start()
+        own_sends(c, begin)
 
     own_gains.wait()
     own_hidden.wait()
@@ -252,42 +297,59 @@
 
         @pl.when(there)
         def _():
-            along_z(plane, up, c).wait_recv()
-            if step < planes - 1:
-
-                @pl.when(onward(up))
-                def _():
-                    along_z(plane, up, c).start()
-
-            over_x(plane, x, c).start()
-            over_y(plane, x, y, c).start()
+            on_z(plane, step, up, c, arrived)
+            first_sends(plane, step, up, c, begin)
 
     def second_hop(step, up, c):
         plane, there = place(step, up)
+        way = ways[step - 1][c]
 
         @pl.when(there)
         def _():
-            over_x(plane, 1 - x, c).wait_recv()
-            second_y(plane, 1 - x, y, c).start()
-            over_y(plane, x, 1 - y, c).wait_recv()
-            second_x(plane, x, 1 - y, c).start()
+            over_x(plane, 1 - x, c, way == "T").wait_recv()
+            if way in "NM":
+                second_y(plane, 1 - x, y, c, way).start()
+                over_y(plane, x, 1 - y, c).wait_recv()
+            if way == "N":
+                second_x(plane, x, 1 - y, c).start()
+            if way == "F":
+                over_y(plane, 1 - x, y, c).start()
             multiply(2 * plane + x, c)
 
     def finish(step, up, c):
         plane, there = place(step, up)
+        way = ways[step - 1][c]
 
         @pl.when(there)
         def _():
-            second_x(plane, 1 - x, 1 - y, c).wait_recv()
-            second_y(plane, 1 - x, 1 - y, c).wait_recv()
+            if way == "N":
+                second_x(plane, 1 - x, 1 - y, c).wait_recv()
+            if way in "NM":
+                second_y(plane, 1 - x, 1 - y, c, way).wait_recv()
+            if way == "F":
+                over_y(plane, 1 - x, 1 - y, c).wait_recv()
             multiply(2 * plane + 1 - x, c)
+
+    def all_sent(step, up, c):
+        plane, there = place(step, up)
+        way = ways[step - 1][c]
+
+        @pl.when(there)
+        def _():
+            first_sends(plane, step, up, c, sent)
+            if way in "NM":
+                second_y(plane, 1 - x, y, c, way).wait_send()
+            if way == "N":
+                second_x(plane, x, 1 - y, c).wait_send()
+            if way == "F":
+                over_y(plane, 1 - x, y, c).wait_send()
 
     slots = (planes - 1) * chunks
     for slot in range(slots + lag + late):
         if slot < slots:
             for up in (True, False):
                 first_hop(slot // chunks + 1, up, slot % chunks)
-        if slot == chunks:
+        if slot == ask:
             for other in range(1, count):
                 to_query(other).start()
         again = slot - lag
@@ -304,12 +366,22 @@
         elif 0 <= last < slots:
             for up in (True, False):
                 finish(last // chunks + 1, up, last % chunks)
+        done = last - 1
+        if -chunks <= done < 0:
+            own_sends(done + chunks, sent)
+            over_y(z, 1 - x, y, done + chunks).wait_send()
+        elif 0 <= done < slots - late:
+            for up in (True, False):
+                all_sent(done // chunks + 1, up, done % chunks)
 
     mine[0] = sum_in[...]
     mine[1] = sum_out[...]
     send_sums = remote(mine, theirs, t_send.at[1], t_recv.at[1], t_peer)
     send_sums.start()
-    send_power.wait_recv()
+    for done in range(slots - late, slots):
+        for up in (True, False):
+            all_sent(done // chunks + 1, up, done % chunks)
+    send_power.wait()
     mean = (power[...] + peer_power[...]) / (2 * hidden.shape[1])
     inverse = lax.rsqrt(mean + EPSILON)[:, :rank]
     own_lengths.wait()
@@ -319,6 +391,8 @@
         remote(
             all_queries.at[dp], all_queries.at[(dp + other) % count], q_send.at[other - 1], q_recv.at[(dp + other) % count], x_peer
         ).wait_recv()
+    for other in range(1, count):
+        to_query(other).wait_send()
     send_sums.wait_recv()
     proj_in = ((mine[0] + theirs[0]) * inverse).astype(jnp.bfloat16)
     proj_out = jnp.where(valid, mine[1] + theirs[1], 0.0).astype(jnp.bfloat16)
@@ -332,8 +406,8 @@
     odd = wide[pl.ds(1, half, stride=2), :]
     lane = lax.broadcasted_iota(jnp.int32, (half, 2 * rank), 1)
     flat = (jnp.where(lane < rank, even, odd) * seq ** (-0.5)).astype(jnp.bfloat16)
-    flat_ref[...] = flat
     flat = flat.astype(jnp.float32)
+    packed_ref[:half, :] = flat
     per_device = all_queries.shape[1]
     score = jnp.zeros((count, per_device, 128), jnp.float32)
     for row in range(half):
@@ -345,40 +419,16 @@
         jnp.int32, (count, per_device, places), 1
     )
     picked = jnp.where(number == ids_ref[...][None], score, 0.0)
-    scores_ref[...] = jnp.sum(jnp.sum(picked, axis=0), axis=0, keepdims=True)
-
-    for c in range(chunks):
-
-        @pl.when(onward(True))
-        def _(c=c):
-            along_z(z, True, c).wait_send()
-
-        @pl.when(onward(False))
-        def _(c=c):
-            along_z(z, False, c).wait_send()
-
-        over_x(z, x, c).wait_send()
-        over_y(z, 1 - x, y, c).wait_send()
-        for step, up in remote_planes:
-            plane, there = place(step, up)
-
-            @pl.when(there)
-            def _(step=step, up=up, plane=plane, c=c):
-                if step < planes - 1:
-
-                    @pl.when(onward(up))
-                    def _():
-                        along_z(plane, up, c).wait_send()
-
-                over_x(plane, x, c).wait_send()
-                over_y(plane, x, y, c).wait_send()
-                second_y(plane, 1 - x, y, c).wait_send()
-                second_x(plane, x, 1 - y, c).wait_send()
-
-    for other in range(1, count):
-        to_query(other).wait_send()
-    send_power.wait_send()
+    packed_ref[half : half + 1, :places] = jnp.sum(jnp.sum(picked, axis=0), axis=0, keepdims=True)
+
     send_sums.wait_send()
+
+
+def lay_out(packed_ref, grads_ref, scores_ref):
+    lines = grads_ref.shape[2] // 128
+    for line in range(lines):
+        grads_ref[0, :, line * 128 : (line + 1) * 128] = packed_ref[line : line + 1, :].astype(jnp.bfloat16)
+    scores_ref[...] = packed_ref[lines : lines + 1, : scores_ref.shape[1]]
 
 
 def local(hidden_states, up_grads, gains, in_bases, out_bases, lengths, queries, query_ids):
@@ -397,18 +447,19 @@
         return gathered_local(hidden_states, up_grads, gains, in_bases, out_bases, lengths, queries, query_ids)
     planes = count // 2
     tiles = (shard_in + shard_out) // 128
-    chunks = 3 if tiles % 3 == 0 else 1
+    fitted = planes - 1 == len(WAYS) and tiles == sum(TILES)
+    widths = tuple(128 * tile for tile in TILES) if fitted else (128 * tiles,)
+    chunks = len(widths)
+    ways = WAYS if fitted else ("N",) * (planes - 1)
+    lag, late, ask = (LAG, LATE, ASK) if fitted else (1, 1, 1)
     hbm, vmem = pl.BlockSpec(memory_space=pltpu.HBM), pl.BlockSpec(memory_space=pltpu.VMEM)
     pairs = pltpu.SemaphoreType.DMA((planes, chunks))
     f32, bf16 = jnp.float32, jnp.bfloat16
-    flat, scores = pl.pallas_call(
-        functools.partial(kernel, planes, chunks, chunks + 1, chunks),
-        out_shape=(
-            jax.ShapeDtypeStruct((rank // 2, 2 * rank), bf16),
-            jax.ShapeDtypeStruct((1, query_ids.shape[0]), f32),
-        ),
+    packed = pl.pallas_call(
+        functools.partial(kernel, planes, widths, ways, lag, late, ask),
+        out_shape=jax.ShapeDtypeStruct((rank // 2 + 8, 2 * rank), f32),
         in_specs=[hbm] * 8,
-        out_specs=(vmem, vmem),
+        out_specs=vmem,
         scratch_shapes=[
             pltpu.VMEM((count, rank, shard_in + shard_out), bf16),
             pltpu.VMEM((seq, width), bf16),
@@ -454,7 +505,15 @@
         queries.reshape(queries.shape[0], -1),
         query_ids.reshape(1, -1),
     )
-    return flat.reshape(1, 1, rank * rank), scores
+    return pl.pallas_call(
+        lay_out,
+        out_shape=(
+            jax.ShapeDtypeStruct((1, 1, rank * rank), bf16),
+            jax.ShapeDtypeStruct((1, query_ids.shape[0]), f32),
+        ),
+        in_specs=[vmem],
+        out_specs=(vmem, vmem),
+    )(packed)
 
 
 def solution(mesh):

time: 36.3 us -> 33.6 us (0.926)
  local copies, waits for them, and re-layouts: 2.45 us -> 0 us
    reshape x1 -> x0, local copies, waits for them, and re-layouts: 1.31 us -> none  [local(): return (flat.reshape(1, 1, rank * rank), scores)]
    unnamed x1 -> x0, local copies, waits for them, and re-layouts: 1.14 us -> none
    pallas_call x1 -> x2, Pallas kernels: 32.4 us -> 32.1 us  [the longest x1 30.7 us: local(): pl.pallas_call(functools.partial(kernel, planes, widths, ways, lag, late,...]
where the time goes in v3:
time: 33.6 us; the launch traced here: 33.4 us
  Pallas kernels  32.1 us (96%)
  between operations  1.29 us (4%)
    pallas_call x1, Pallas kernels, local(): pl.pallas_call(functools.partial(kernel, planes, widths, ways, lag, late,...  30.7 us
    pallas_call x1, Pallas kernels, local(): pl.pallas_call(lay_out, out_shape=(jax.ShapeDtypeStruct((1, 1, rank * ran...  1.36 us

profile of v3, /device:TPU:1, one launch (start us, length us, event | category | flops | bytes accessed | tf_op | source)
XLA Modules:
  0.0 33.4 jit_solution(13726530500875890889)
XLA Ops:
  1.3 30.7 %shard_map.95.packed_ref = f32[40,128]{1,0:T(8,128)} custom-call(bf16[128,4096]{1,0:T(8,128)(2,1)} %bitcast.11, bf16[128,14336]{1,0:T(8,128)(2,1)} %bitcast.10, bf16[1,4096]{1,0:T(2,128)(2,1)} %gains_hbm.1, bf16[64,512]{1,0:T(8,128)(2,1)} %bitcast.13, bf16[64,1792]{1,0:T(8,128)(2,1)} %bitcast.12, s32[1]{0:T(128)S(6)} %copy.10.lengths_hbm, ...), custom_call_target="tpu_custom_call" | custom-call | tf_op jit(solution)/shard_map/pallas_call | solution.py:458
  32.0 1.4 %shard_map.96 = (bf16[1,1,4096]{2,1,0:T(2,128)(2,1)}, f32[1,16]{1,0:T(1,128)}) custom-call(f32[40,128]{1,0:T(8,128)} %shard_map.95.packed_ref), custom_call_target="tpu_custom_call" | custom-call | tf_op jit(solution)/shard_map/pallas_call | solution.py:508

commit v4 on v3

--- a/solution.py
+++ b/solution.py
@@ -68,7 +68,7 @@
     return (example_grads, scores)
 
 WAYS = ("NMT", "MMT", "MNT")
-TILES = (6, 6, 6)
+TILES = (7, 5, 6)
 LAG, LATE, ASK = 3, 5, 3
 
 

time: 33.6 us -> 33.5 us (level)
  no operation moved by 1% of the time
where the time goes in v4:
time: 33.5 us; the launch traced here: 33.3 us
  Pallas kernels  32 us (96%)
  between operations  1.29 us (4%)
    pallas_call x1, Pallas kernels, local(): pl.pallas_call(functools.partial(kernel, planes, widths, ways, lag, late,...  30.7 us
    pallas_call x1, Pallas kernels, local(): pl.pallas_call(lay_out, out_shape=(jax.ShapeDtypeStruct((1, 1, rank * ran...  1.36 us

profile of v4, /device:TPU:1, one launch (start us, length us, event | category | flops | bytes accessed | tf_op | source)
XLA Modules:
  0.0 33.3 jit_solution(17888862421279488063)
XLA Ops:
  1.3 30.7 %shard_map.95.packed_ref = f32[40,128]{1,0:T(8,128)} custom-call(bf16[128,4096]{1,0:T(8,128)(2,1)} %bitcast.11, bf16[128,14336]{1,0:T(8,128)(2,1)} %bitcast.10, bf16[1,4096]{1,0:T(2,128)(2,1)} %gains_hbm.1, bf16[64,512]{1,0:T(8,128)(2,1)} %bitcast.13, bf16[64,1792]{1,0:T(8,128)(2,1)} %bitcast.12, s32[1]{0:T(128)S(6)} %copy.10.lengths_hbm, ...), custom_call_target="tpu_custom_call" | custom-call | tf_op jit(solution)/shard_map/pallas_call | solution.py:458
  31.9 1.4 %shard_map.96 = (bf16[1,1,4096]{2,1,0:T(2,128)(2,1)}, f32[1,16]{1,0:T(1,128)}) custom-call(f32[40,128]{1,0:T(8,128)} %shard_map.95.packed_ref), custom_call_target="tpu_custom_call" | custom-call | tf_op jit(solution)/shard_map/pallas_call | solution.py:508
